TPU v7x, 512 devices: a whole 4x8x8 slice. The times are simulated.
512 devices in a mesh: dp: 8 (over y), ctx: 16 (over z_hi, x, core), head: 4 (over z_lo).
Axes of the slice: x: 4, y: 8, z: 8 (z_hi: 2, z_lo: 4; z = z_hi * 4 + z_lo), core: 2. Of those that a mesh axis runs over, the one named last changes fastest.
Arguments:
- queries: bfloat16 [65536, 3072], P(('dp', 'ctx'), 'head'), parts along dimension 0, may hold values from -6 to 6
- keys: bfloat16 [65536, 3072], P(('dp', 'ctx'), 'head'), parts along dimension 0, may hold values from -8 to 8
- values: bfloat16 [65536, 3072], P(('dp', 'ctx'), 'head'), parts along dimension 0, may hold values from -8 to 8
- pool_segments: int32 [128, 512], P(('dp', 'ctx')), parts along dimension 0, may hold values from 0 to 7, never falling along the last dimension, each value on 1 to 96 neighbouring positions
- window_map: int32 [128], P(('dp', 'ctx')), parts along dimension 0, may hold values from 0 to 15, each once
- ref_owner: int32 [8], P('dp'), parts along dimension 0, may hold values from 0 to 15
- ref_keys: bfloat16 [128, 512, 3072], P(('dp', 'ctx'), 'head'), parts along dimension 0, may hold values from -6 to 6
- ref_values: bfloat16 [128, 512, 3072], P(('dp', 'ctx'), 'head'), parts along dimension 0, may hold values from -6 to 6
- slopes: float32 [24], P('head'), may hold values from 0.02 to 2
Outputs:
- attended: bfloat16 [65536, 3072], P(('dp', 'ctx'), 'head'), parts along dimension 0
There are 8 independent parts, one for each index of `dp`. A program takes and returns all parts, laid end to end along the dimension named above; an argument that names none is the same for every part. Nothing has to cross between parts.
All inputs are finite; a program needn't handle non-finite values.
Results may differ from a plain program's by a relative error of at most 0.0021.
Values may be sent and summed in bfloat16 or wider, within the bound.
No kernel may reach another device: no remote copies, remote signals or barrier semaphores. Data moves between devices by JAX's collectives and lax.ppermute only.
A program may use at most 64 MiB of HBM per device.

v0:
```python
from functools import reduce
import math
import jax
import jax.numpy as jnp
from jax import lax
from jax.sharding import PartitionSpec as P

HD = 128
RATIO = 64


def spread(block, axis, source):
    block = jnp.where(lax.axis_index(axis) == source, block, jnp.zeros_like(block))
    return lax.psum(block, axis)


def group_terms(query_block, key_block, value_block, bias_term):
    score_scale = 1.0 / math.sqrt(HD)
    scores = (
        jnp.einsum("qhd,khd->hqk", query_block, key_block, preferred_element_type=jnp.float32)
        * score_scale
    )
    if bias_term is not None:
        scores = scores + bias_term[:, None, :]
    row_max = jnp.max(scores, axis=2)
    exp_terms = jnp.exp(scores - row_max[:, :, None])
    row_total = jnp.sum(exp_terms, axis=2)
    weights = exp_terms.astype(jnp.bfloat16)
    numerator = jnp.einsum("hqk,khd->qhd", weights, value_block, preferred_element_type=jnp.float32)
    return (row_max.T, row_total.T, numerator)


def combine_groups(group_list):
    ceiling = reduce(jnp.maximum, [triple[0] for triple in group_list])
    numerator = reduce(
        jnp.add, [jnp.exp(triple[0] - ceiling)[:, :, None] * triple[2] for triple in group_list]
    )
    denominator = reduce(
        jnp.add, [jnp.exp(triple[0] - ceiling) * triple[1] for triple in group_list]
    )
    return numerator / denominator[:, :, None]


def on_device(
    queries, keys, values, pool_segments, window_map, ref_owner, ref_keys, ref_values, slopes
):
    tok_rows = queries.shape[0]
    heads_here = queries.shape[1] // HD
    pool_count = tok_rows // RATIO
    member = (pool_segments[0][None, :] == jnp.arange(pool_count, dtype=jnp.int32)[:, None]).astype(
        jnp.bfloat16
    )
    counts = jnp.sum(member, axis=1, dtype=jnp.float32)
    pooled_keys = (
        jnp.dot(member, keys, preferred_element_type=jnp.float32) / counts[:, None]
    ).astype(jnp.bfloat16)
    pooled_values = (
        jnp.dot(member, values, preferred_element_type=jnp.float32) / counts[:, None]
    ).astype(jnp.bfloat16)
    window_tag = window_map.astype(jnp.bfloat16)
    all_keys, all_values, all_tags = (
        lax.all_gather(pooled_keys, "ctx", axis=0, tiled=True),
        lax.all_gather(pooled_values, "ctx", axis=0, tiled=True),
        lax.all_gather(window_tag, "ctx", axis=0, tiled=True),
    )
    ref_k, ref_v = (
        spread(ref_keys[0], "ctx", ref_owner[0]),
        spread(ref_values[0], "ctx", ref_owner[0]),
    )
    ref_k, ref_v = (
        lax.all_to_all(ref_k, "head", split_axis=1, concat_axis=0, tiled=True),
        lax.all_to_all(ref_v, "head", split_axis=1, concat_axis=0, tiled=True),
    )
    query_block = queries.reshape(tok_rows, heads_here, HD)
    key_block = keys.reshape(tok_rows, heads_here, HD)
    value_block = values.reshape(tok_rows, heads_here, HD)
    key_window = jnp.repeat(all_tags.astype(jnp.float32), pool_count)
    distance = jnp.abs(window_map[0].astype(jnp.float32) - key_window)
    bias_term = -slopes[:, None] * distance[None, :]
    group_list = [
        group_terms(query_block, key_block, value_block, None),
        group_terms(
            query_block,
            all_keys.reshape(-1, heads_here, HD),
            all_values.reshape(-1, heads_here, HD),
            bias_term,
        ),
        group_terms(
            query_block, ref_k.reshape(-1, heads_here, HD), ref_v.reshape(-1, heads_here, HD), None
        ),
    ]
    merged = combine_groups(group_list)
    return merged.reshape(tok_rows, heads_here * HD).astype(jnp.bfloat16)


def solution(mesh):
    return jax.shard_map(
        on_device,
        mesh=mesh,
        in_specs=(
            P(("dp", "ctx"), "head"),
            P(("dp", "ctx"), "head"),
            P(("dp", "ctx"), "head"),
            P(("dp", "ctx"), None),
            P(("dp", "ctx")),
            P("dp"),
            P(("dp", "ctx"), "head", None),
            P(("dp", "ctx"), "head", None),
            P("head"),
        ),
        out_specs=P(("dp", "ctx"), "head"),
        check_vma=False,
    )
```

profile of v0, /device:TPU:1, one launch (start us, length us, event | category | flops | bytes accessed | tf_op | source)
XLA Modules:
  0.0 324.7 jit_solution(16259391540248916373)
XLA Ops:
  6.5 0.0 all-reduce.4.cloned.1.call-start
  7.2 0.1 broadcast_select_fusion
  7.3 0.0 copy-start.7
  7.3 0.0 copy-start.1
  7.3 0.0 copy-start.6
  7.4 1.2 copy.74
  8.5 1.1 copy.65
  9.7 0.0 copy-start.4
  9.7 0.0 all-reduce.4.cloned.1.call-update
  10.4 1.3 dynamic-slice
  11.8 0.7 dynamic-update-slice
  12.5 49.1 %all-reduce = bf16[16]{0:T(256)(128)(2,1)S(1)} all-reduce(bf16[16]{0:T(256)(128)(2,1)S(1)} %dynamic-update-slice), channel_id=1, replica_groups=mesh['dp'=8,'ctx'=16,'head'=4] {'ctx'}, use_global_device_ids=true, to_apply=%add | all-reduce | flops 16 | bytes 64
  61.6 0.0 copy-done.7
  61.6 0.1 broadcast_in_dim.2
  61.7 0.1 abs.12
  61.8 0.0 copy-done.1
  61.8 1.3 copy.59
  63.0 0.0 copy-done.6
  63.0 0.1 convert_reduce_fusion
  63.1 141.0 %all-reduce.4.cloned.1.call-done = (bf16[128,4,768]{0,2,1:T(8,128)(2,1)}, bf16[128,4,768]{0,2,1:T(8,128)(2,1)}) async-done(((bf16[128,4,768]{0,2,1:T(8,128)(2,1)}, bf16[128,4,768]{0,2,1:T(8,128)(2,1)}), (bf16[128,4,768]{0,2,1:T(8,128)(2,1)}, bf16[128,4,768]{0,2,1:T(8,128)(2,1)})) %all-reduce.4.cloned.1.call-update) | async-done | bytes 1572880 | tf_op jit(solution)/shard_map/psum | solution.py:14
  204.2 4.2 %all-to-all-start.1 = ((bf16[128,4,768]{0,2,1:T(8,128)(2,1)}), bf16[128,4,768]{0,2,1:T(8,128)(2,1)}, u32[]{:S(2)}, u32[]{:S(2)}) async-start(bf16[128,4,768]{0,2,1:T(8,128)(2,1)} %get-tuple-element.5), calls=%async_computation.1 | async-start | bytes 1572864 | tf_op jit(solution)/shard_map/all_to_all | solution.py:72
  208.4 0.2 fusion.20
  208.6 36.4 %all_gather.9 = bf16[128,768]{1,0:T(8,128)(2,1)S(1)} all-gather(bf16[8,768]{1,0:T(8,128)(2,1)S(1)} %fusion.20), channel_id=1, replica_groups=mesh['dp'=8,'ctx'=16,'head'=4] {'ctx'}, dimensions={0}, use_global_device_ids=true | all-gather | bytes 208896 | tf_op jit(solution)/shard_map/all_gather | solution.py:62
  245.0 0.2 copy.62
  245.1 0.0 copy-done.4
  245.1 0.3 copy.58
  245.4 0.1 broadcast_multiply_fusion
  245.5 1.0 bitcast_reduce_fusion.1
  246.5 0.0 copy-start.2
  246.5 4.9 %multiply_reduce_fusion = (f32[6,512]{1,0:T(8,128)S(1)}, f32[6,512,512]{1,2,0:T(8,128)}) fusion(bf16[512,6,128]{0,2,1:T(8,128)(2,1)S(1)} %bitcast.127, bf16[512,6,128]{0,2,1:T(8,128)(2,1)} %bitcast.132), kind=kOutput, calls=%fused_computation.4 | convolution fusion | flops 405795840 | bytes 7876608 | tf_op jit(solution)/shard_map/qhd,khd->hqk/dot_general | solution.py:20
  251.4 0.0 all-to-all-done.1
  251.4 4.5 %all-to-all-start = ((bf16[128,4,768]{0,2,1:T(8,128)(2,1)}), bf16[128,4,768]{0,2,1:T(8,128)(2,1)}, u32[]{:S(2)}, u32[]{:S(2)}) async-start(bf16[128,4,768]{0,2,1:T(8,128)(2,1)} %get-tuple-element.6), calls=%async_computation | async-start | bytes 1572864 | tf_op jit(solution)/shard_map/all_to_all | solution.py:71
  255.9 0.0 copy-done.2
  255.9 0.2 fusion.21
  256.1 1.4 copy.70
  257.5 35.2 %all_gather.11 = bf16[128,768]{1,0:T(8,128)(2,1)S(1)} all-gather(bf16[8,768]{1,0:T(8,128)(2,1)S(1)} %fusion.21), channel_id=1, replica_groups=mesh['dp'=8,'ctx'=16,'head'=4] {'ctx'}, dimensions={0}, use_global_device_ids=true | all-gather | bytes 208896 | tf_op jit(solution)/shard_map/all_gather | solution.py:63
  292.8 0.2 copy.72
  292.9 1.0 fusion.18
  293.9 0.0 copy-start
  293.9 4.0 %fusion.1 = f32[6,512]{1,0:T(8,128)S(1)} fusion(f32[6,512,512]{1,2,0:T(8,128)} %get-tuple-element.14, f32[6,512]{1,0:T(8,128)S(1)} %get-tuple-element.13), kind=kLoop, calls=%fused_computation.5 | loop fusion | flops 4715520 | bytes 6316032 | tf_op jit(solution)/shard_map/reduce_sum | solution.py:27
  297.9 0.6 copy-done
  298.5 2.5 fusion.7
  300.9 2.6 copy.75
  303.6 1.6 reshape.86
  305.2 0.0 all-to-all-done
  305.2 2.6 copy.66
  307.9 2.4 reshape.83
  310.2 2.2 bitcast_reduce_fusion
  312.5 1.6 fusion.3
  314.1 0.0 copy-start.5
  314.1 0.0 copy-start.3
  314.1 1.9 fusion.5
  316.0 0.0 copy-done.5
  316.1 0.0 copy-done.3
  316.1 0.6 fusion.15
  316.7 1.2 copy.76
  (4 shorter events, 0.0 us)
Async XLA Ops:
  6.5 197.6 %all-reduce.4.cloned.1.call-start = ((), (), s32[]{:S(2)}) async-start(), calls=%async_computation.2 | async-start | bytes 3145728 | tf_op jit(solution)/shard_map/psum | solution.py:14
  7.3 54.3 %copy-start.7 = (f32[6]{0:T(128)S(1)}, f32[6]{0:T(128)}, u32[]{:S(2)}) copy-start(f32[6]{0:T(128)} %param.17) | copy-start | bytes 76
  7.3 54.4 %copy-start.1 = (bf16[512,768]{1,0:T(8,128)(2,1)S(1)}, bf16[512,768]{1,0:T(8,128)(2,1)}, u32[]{:S(2)}) copy-start(bf16[512,768]{1,0:T(8,128)(2,1)} %param.10) | copy-start | bytes 2359300
  7.3 55.7 %copy-start.6 = (s32[1,512]{1,0:T(1,128)S(1)}, s32[1,512]{1,0:T(1,128)}, u32[]{:S(2)}) copy-start(s32[1,512]{1,0:T(1,128)} %param.12) | copy-start | bytes 6148
  9.7 235.5 %copy-start.4 = (bf16[512,768]{1,0:T(8,128)(2,1)S(1)}, bf16[512,768]{1,0:T(8,128)(2,1)}, u32[]{:S(2)}) copy-start(bf16[512,768]{1,0:T(8,128)(2,1)} %param.9) | copy-start | bytes 2359300
  204.2 47.2 %all-to-all-start.1 = ((bf16[128,4,768]{0,2,1:T(8,128)(2,1)}), bf16[128,4,768]{0,2,1:T(8,128)(2,1)}, u32[]{:S(2)}, u32[]{:S(2)}) async-start(bf16[128,4,768]{0,2,1:T(8,128)(2,1)} %get-tuple-element.5), calls=%async_computation.1 | async-start | bytes 1572864 | tf_op jit(solution)/shard_map/all_to_all | solution.py:72
  246.5 9.4 %copy-start.2 = (bf16[512,768]{1,0:T(8,128)(2,1)S(1)}, bf16[512,768]{1,0:T(8,128)(2,1)}, u32[]{:S(2)}) copy-start(bf16[512,768]{1,0:T(8,128)(2,1)} %param.11) | copy-start | bytes 2359300
  251.4 53.8 %all-to-all-start = ((bf16[128,4,768]{0,2,1:T(8,128)(2,1)}), bf16[128,4,768]{0,2,1:T(8,128)(2,1)}, u32[]{:S(2)}, u32[]{:S(2)}) async-start(bf16[128,4,768]{0,2,1:T(8,128)(2,1)} %get-tuple-element.6), calls=%async_computation | async-start | bytes 1572864 | tf_op jit(solution)/shard_map/all_to_all | solution.py:71
  293.9 4.6 %copy-start = (f32[6,512,512]{1,2,0:T(8,128)S(1)}, f32[6,512,512]{1,2,0:T(8,128)}, u32[]{:S(2)}) copy-start(f32[6,512,512]{1,2,0:T(8,128)} %get-tuple-element.14) | copy-start | bytes 18874372
  314.1 2.0 copy-start.5
  314.1 2.0 copy-start.3
Sparse Core Ops, SparseCore 0:
  10.3 193.8 all-reduce.3
where the time goes:
time: 325 us
  waiting for transfers between devices  141 us (43%)
  blocking collectives  121 us (37%)
  local copies, waits for them, and re-layouts  18.9 us (6%)
  between operations  15 us (5%)
  matrix products  13.6 us (4%)
  starting transfers between devices  8.65 us (3%)
  other arithmetic  6.88 us (2%)
    psum x1, waiting for transfers between devices, spread(): return lax.psum(block, axis)  141 us
    unnamed x1, blocking collectives  49.1 us
    all_gather x1, blocking collectives, on_device(): lax.all_gather(pooled_keys, 'ctx', axis=0, tiled=True)  36.4 us
    all_gather x1, blocking collectives, on_device(): lax.all_gather(pooled_values, 'ctx', axis=0, tiled=True)  35.2 us
    dot_general x3, matrix products, group_terms(): jnp.einsum('qhd,khd->hqk', query_block, key_block, preferred_element_type...  8.16 us
    reduce_sum x3, other arithmetic, group_terms(): row_total = jnp.sum(exp_terms, axis=2)  6.54 us
  transfers between devices with their start and end apart: 3, of which 1 were waited for; matrix products, arithmetic and copies ran while one was open for 7% of the time, Pallas kernels for 0%

commit v1 on v0

--- a/solution.py
+++ b/solution.py
@@ -11,7 +11,7 @@
 
 def spread(block, axis, source):
     block = jnp.where(lax.axis_index(axis) == source, block, jnp.zeros_like(block))
-    return lax.psum(block, axis)
+    return jnp.sum(lax.all_gather(block, axis), axis=0)
 
 
 def group_terms(query_block, key_block, value_block, bias_term):

time: 325 us -> 399 us (1.23)
  waiting for transfers between devices: 141 us -> 181 us
  other arithmetic: 6.88 us -> 25.9 us
  blocking collectives: 121 us -> 137 us
    all_gather x0 -> x2, waiting for transfers between devices: none -> 181 us  [spread(): return jnp.sum(lax.all_gather(block, axis), axis=0)]
    psum x1 -> x0, waiting for transfers between devices: 141 us -> none  [spread(): return lax.psum(block, axis)]
    all_gather x1, blocking collectives: 36.4 us -> 53.9 us  [on_device(): lax.all_gather(pooled_keys, 'ctx', axis=0, tiled=True)]
    reduce_sum x0 -> x2, other arithmetic: none -> 15.7 us  [spread(): return jnp.sum(lax.all_gather(block, axis), axis=0)]
  transfers between devices with their start and end apart: 3 -> 4, of which waited for: 1 -> 2; matrix products, arithmetic and copies ran while one was open for 7% -> 12% of each run, Pallas kernels for 0% -> 0%
where the time goes in v1:
time: 399 us
  waiting for transfers between devices  181 us (45%)
  blocking collectives  137 us (34%)
  other arithmetic  25.9 us (6%)
  local copies, waits for them, and re-layouts  17.4 us (4%)
  between operations  14.9 us (4%)
  matrix products  14 us (4%)
  starting transfers between devices  8.42 us (2%)
    all_gather x2, waiting for transfers between devices, spread(): return jnp.sum(lax.all_gather(block, axis), axis=0)  181 us
    all_gather x1, blocking collectives, on_device(): lax.all_gather(pooled_keys, 'ctx', axis=0, tiled=True)  53.9 us
    unnamed x1, blocking collectives  49.9 us
    all_gather x1, blocking collectives, on_device(): lax.all_gather(pooled_values, 'ctx', axis=0, tiled=True)  32.9 us
    reduce_sum x2, other arithmetic, spread(): return jnp.sum(lax.all_gather(block, axis), axis=0)  15.7 us
  transfers between devices with their start and end apart: 4, of which 2 were waited for; matrix products, arithmetic and copies ran while one was open for 12% of the time, Pallas kernels for 0%

profile of v1, /device:TPU:1, one launch (start us, length us, event | category | flops | bytes accessed | tf_op | source)
XLA Modules:
  0.0 398.7 jit_solution(6772705238311208215)
XLA Ops:
  6.5 0.0 copy-start.4
  6.5 0.0 all-gather.3.cloned.1.call-start
  7.2 1.0 broadcast_select_fusion.1
  8.2 0.0 all-gather.3.cloned.1.call-update
  8.2 0.0 all-gather.5.cloned.1.call-start
  8.3 0.9 broadcast_select_fusion
  9.2 0.0 all-gather.5.cloned.1.call-update
  9.9 1.3 dynamic-slice
  11.2 0.7 dynamic-update-slice
  11.9 49.9 %all-reduce = bf16[16]{0:T(256)(128)(2,1)S(1)} all-reduce(bf16[16]{0:T(256)(128)(2,1)S(1)} %dynamic-update-slice), channel_id=1, replica_groups=mesh['dp'=8,'ctx'=16,'head'=4] {'ctx'}, use_global_device_ids=true, to_apply=%add | all-reduce | flops 16 | bytes 64
  61.8 0.7 neg.4
  62.5 0.1 broadcast_in_dim.2
  62.6 0.1 abs.12
  62.7 1.4 copy.74
  64.1 0.0 copy-done.4
  64.1 0.1 convert_reduce_fusion
  64.2 0.0 copy-start.2
  64.2 99.9 %all-gather.3.cloned.1.call-done = bf16[16,128,3072]{2,1,0:T(8,128)(2,1)} async-done(((bf16[1,128,3072]{2,1,0:T(8,128)(2,1)}), bf16[16,128,3072]{2,1,0:T(8,128)(2,1)}) %all-gather.3.cloned.1.call-update) | async-done | bytes 12582928 | tf_op jit(solution)/shard_map/all_gather | solution.py:14
  164.1 7.4 %reduce_sum.61 = bf16[128,3072]{1,0:T(8,128)(2,1)S(1)} reduce(bf16[16,128,3072]{2,1,0:T(8,128)(2,1)} %all-gather.3.cloned.1.call-done, bf16[]{:T(256)} %constant.16.clone.1), dimensions={0}, to_apply=%region_3.4 | reduce | flops 5898240 | bytes 13369346 | tf_op jit(solution)/shard_map/reduce_sum | solution.py:14
  171.5 1.2 copy.80
  172.7 4.2 %all-to-all-start = ((bf16[128,4,768]{0,2,1:T(8,128)(2,1)}), bf16[128,4,768]{0,2,1:T(8,128)(2,1)}, u32[]{:S(2)}, u32[]{:S(2)}) async-start(bf16[128,4,768]{0,2,1:T(8,128)(2,1)} %bitcast.10), calls=%async_computation | async-start | bytes 1572864 | tf_op jit(solution)/shard_map/all_to_all | solution.py:71
  176.9 0.0 copy-done.2
  176.9 0.2 fusion.20
  177.1 53.9 %all_gather.17 = bf16[128,768]{1,0:T(8,128)(2,1)S(1)} all-gather(bf16[8,768]{1,0:T(8,128)(2,1)S(1)} %fusion.20), channel_id=1, replica_groups=mesh['dp'=8,'ctx'=16,'head'=4] {'ctx'}, dimensions={0}, use_global_device_ids=true | all-gather | bytes 208896 | tf_op jit(solution)/shard_map/all_gather | solution.py:62
  231.0 0.2 copy.77
  231.1 1.4 copy.73
  232.5 0.1 broadcast_multiply_fusion
  232.6 1.6 bitcast_reduce_fusion.1
  234.2 3.6 multiply_reduce_fusion
  237.8 81.4 %all-gather.5.cloned.1.call-done = bf16[16,128,3072]{2,1,0:T(8,128)(2,1)} async-done(((bf16[1,128,3072]{2,1,0:T(8,128)(2,1)}), bf16[16,128,3072]{2,1,0:T(8,128)(2,1)}) %all-gather.5.cloned.1.call-update) | async-done | bytes 12582928 | tf_op jit(solution)/shard_map/all_gather | solution.py:14
  319.2 8.4 %reduce_sum.62 = bf16[128,3072]{1,0:T(8,128)(2,1)} reduce(bf16[16,128,3072]{2,1,0:T(8,128)(2,1)} %all-gather.5.cloned.1.call-done, bf16[]{:T(256)} %constant.16.clone.1), dimensions={0}, to_apply=%region_5.6 | reduce | flops 5898240 | bytes 13369346 | tf_op jit(solution)/shard_map/reduce_sum | solution.py:14
  327.6 0.0 slice-start
  327.6 2.4 copy.89
  330.0 0.0 all-to-all-done
  330.1 4.2 %all-to-all-start.1 = ((bf16[128,4,768]{0,2,1:T(8,128)(2,1)}), bf16[128,4,768]{0,2,1:T(8,128)(2,1)}, u32[]{:S(2)}, u32[]{:S(2)}) async-start(bf16[128,4,768]{0,2,1:T(8,128)(2,1)} %bitcast.132), calls=%async_computation.1 | async-start | bytes 1572864 | tf_op jit(solution)/shard_map/all_to_all | solution.py:72
  334.2 1.3 fusion.21
  335.6 2.3 copy.85
  337.9 32.9 %all_gather.20 = bf16[128,768]{1,0:T(8,128)(2,1)S(1)} all-gather(bf16[8,768]{1,0:T(8,128)(2,1)S(1)} %fusion.21), channel_id=1, replica_groups=mesh['dp'=8,'ctx'=16,'head'=4] {'ctx'}, dimensions={0}, use_global_device_ids=true | all-gather | bytes 208896 | tf_op jit(solution)/shard_map/all_gather | solution.py:63
  370.8 0.2 copy.87
  371.0 0.0 copy-start.1
  371.0 0.0 slice-start.1
  371.0 1.8 fusion.18
  372.8 4.0 fusion.1
  376.8 0.0 slice-done
  376.8 0.0 copy-done.1
  376.8 0.0 slice-done.1
  376.8 2.5 fusion.7
  379.3 1.7 copy.81
  381.0 1.2 reshape.77
  382.2 0.0 all-to-all-done.1
  382.2 1.7 copy.90
  384.0 0.3 reshape.80
  384.3 2.2 bitcast_reduce_fusion
  386.5 0.0 copy-start
  386.5 0.0 copy-start.3
  386.5 1.6 fusion.3
  388.1 1.9 fusion.5
  390.1 0.0 copy-done
  390.1 0.0 copy-done.3
  390.1 0.6 fusion.15
  390.7 1.2 copy.91
  (4 shorter events, 0.0 us)
Async XLA Ops:
  6.5 57.5 %copy-start.4 = (s32[1,512]{1,0:T(1,128)S(1)}, s32[1,512]{1,0:T(1,128)}, u32[]{:S(2)}) copy-start(s32[1,512]{1,0:T(1,128)} %param.12) | copy-start | bytes 6148
  6.5 157.6 %all-gather.3.cloned.1.call-start = ((), (), s32[]{:S(2)}) async-start(), calls=%async_computation.2 | async-start | bytes 13369344 | tf_op jit(solution)/shard_map/all_gather | solution.py:14
  8.2 311.0 %all-gather.5.cloned.1.call-start = ((), (), s32[]{:S(2)}) async-start(), calls=%async_computation.3 | async-start | bytes 13369344 | tf_op jit(solution)/shard_map/all_gather | solution.py:14
  64.2 112.7 %copy-start.2 = (bf16[512,768]{1,0:T(8,128)(2,1)S(1)}, bf16[512,768]{1,0:T(8,128)(2,1)}, u32[]{:S(2)}) copy-start(bf16[512,768]{1,0:T(8,128)(2,1)} %param.10) | copy-start | bytes 2359300
  172.7 157.4 %all-to-all-start = ((bf16[128,4,768]{0,2,1:T(8,128)(2,1)}), bf16[128,4,768]{0,2,1:T(8,128)(2,1)}, u32[]{:S(2)}, u32[]{:S(2)}) async-start(bf16[128,4,768]{0,2,1:T(8,128)(2,1)} %bitcast.10), calls=%async_computation | async-start | bytes 1572864 | tf_op jit(solution)/shard_map/all_to_all | solution.py:71
  327.6 49.2 %slice-start = ((s8[6291456]{0:T(1024)(128)(4,1)}), s8[2097152]{0:T(1024)(128)(4,1)S(1)}, s32[]{:S(2)}) async-start(s8[6291456]{0:T(1024)(128)(4,1)} %bitcast.126), calls=%async_computation.4 | async-start | bytes 4194304
  330.1 52.2 %all-to-all-start.1 = ((bf16[128,4,768]{0,2,1:T(8,128)(2,1)}), bf16[128,4,768]{0,2,1:T(8,128)(2,1)}, u32[]{:S(2)}, u32[]{:S(2)}) async-start(bf16[128,4,768]{0,2,1:T(8,128)(2,1)} %bitcast.132), calls=%async_computation.1 | async-start | bytes 1572864 | tf_op jit(solution)/shard_map/all_to_all | solution.py:72
  371.0 5.8 %copy-start.1 = (bf16[512,768]{0,1:T(8,128)(2,1)S(1)}, bf16[512,768]{0,1:T(8,128)(2,1)}, u32[]{:S(2)}) copy-start(bf16[512,768]{0,1:T(8,128)(2,1)} %copy.85) | copy-start | bytes 2359300
  371.0 5.8 %slice-start.1 = ((s8[6291456]{0:T(1024)(128)(4,1)}), s8[4194304]{0:T(1024)(128)(4,1)S(1)}, s32[]{:S(2)}) async-start(s8[6291456]{0:T(1024)(128)(4,1)} %bitcast.126), calls=%async_computation.5 | async-start | bytes 8388608
  386.5 3.6 copy-start
  386.5 3.6 copy-start.3
Sparse Core Ops, SparseCore 0:
  10.7 153.4 all-gather.2
  167.4 151.7 all-gather.4
